TPU v7x, 256 devices: a whole 4x4x8 slice. The times are simulated.
256 devices in a mesh: theta: 64 (over y_lo, x, z), row: 4 (over y_hi, core).
Axes of the slice: x: 4, y: 4 (y_hi: 2, y_lo: 2; y = y_hi * 2 + y_lo), z: 8, core: 2. Of those that a mesh axis runs over, the one named last changes fastest.
Arguments:
- velocity: float32 [3, 512, 1536, 128], P(None, 'theta', 'row'), may hold values from -5 to 5
Outputs:
- radial_part: bfloat16 [3, 512, 1536, 128], P(None, 'theta', 'row')
- azimuthal_part: bfloat16 [3, 512, 1536, 128], P(None, 'theta', 'row')
All inputs are finite; a program needn't handle non-finite values.
Results may differ from a plain program's by a relative error of at most 0.001.
Values sent between devices are 32-bit elements; how exact they have to be, the bound alone decides.
A program may use at most 192 MiB of HBM per device.

v0:
```python
import math

import jax
import jax.numpy as jnp
from jax import lax
from jax.sharding import PartitionSpec as P


def extended(cells, sides, width, closed):
    for axis, dim in sides:
        count = lax.axis_size(axis)
        ends = count if closed else count - 1
        head = lax.slice_in_dim(cells, 0, width, axis=dim)
        tail = lax.slice_in_dim(cells, cells.shape[dim] - width, cells.shape[dim], axis=dim)
        cells = jnp.concatenate(
            [
                lax.ppermute(tail, axis, [(i, (i + 1) % count) for i in range(ends)]),
                cells,
                lax.ppermute(head, axis, [((i + 1) % count, i) for i in range(ends)]),
            ],
            axis=dim,
        )
    return cells


def shifted(x, axis, by):
    peers = lax.axis_size(axis)
    return lax.ppermute(x, axis, [(i, (i + by) % peers) for i in range(peers)])


def tendencies(velocity, radial_ext, azimuth_ext, shell_pos, grid_r, grid_t):
    spacing = 1.0 / grid_r
    angle_step = 2.0 * math.pi / grid_t
    axial_step = 4.0 / grid_r
    viscosity = 0.5 / grid_r
    time_step = 0.2 / grid_r
    angle_time = 2.0 / grid_r
    radius = (shell_pos + 0.5) * spacing
    radial_slope = (
        8.0 * (radial_ext[:, :, 3:-1] - radial_ext[:, :, 1:-3])
        - (radial_ext[:, :, 4:] - radial_ext[:, :, :-4])
    ) / (12.0 * spacing)
    radial_lap = (
        (shell_pos + 1.0) * (radial_ext[:, :, 3:-1] - velocity)
        - shell_pos * (velocity - radial_ext[:, :, 1:-3])
    ) / ((shell_pos + 0.5) * spacing * spacing)
    angle_slope = (
        8.0 * (azimuth_ext[:, 3:-1] - azimuth_ext[:, 1:-3])
        - (azimuth_ext[:, 4:] - azimuth_ext[:, :-4])
    ) / (12.0 * angle_step)
    angle_lap = (azimuth_ext[:, 3:-1] - 2.0 * velocity + azimuth_ext[:, 1:-3]) / (
        angle_step * angle_step
    )
    ahead_one = jnp.roll(velocity, -1, axis=3)
    behind_one = jnp.roll(velocity, 1, axis=3)
    ahead_two = jnp.roll(velocity, -2, axis=3)
    behind_two = jnp.roll(velocity, 2, axis=3)
    axial_slope = (8.0 * (ahead_one - behind_one) - (ahead_two - behind_two)) / (12.0 * axial_step)
    axial_lap = (ahead_one - 2.0 * velocity + behind_one) / (axial_step * axial_step)
    u_rad = velocity[0]
    u_ang = velocity[1]
    u_ax = velocity[2]
    radial_part = time_step * (
        -(u_rad * radial_slope + u_ax * axial_slope) + viscosity * (radial_lap + axial_lap)
    )
    zeros = jnp.zeros_like(u_rad)
    curvature = jnp.stack([radius * u_ang * u_ang, -radius * u_rad * u_ang, zeros])
    metric = jnp.stack([-u_rad - 2.0 * angle_slope[1], -u_ang + 2.0 * angle_slope[0], zeros])
    azimuthal_part = angle_time * (
        -radius * u_ang * angle_slope + curvature + viscosity * (angle_lap + metric)
    )
    return (radial_part.astype(jnp.bfloat16), azimuthal_part.astype(jnp.bfloat16))


def per_device(velocity):
    width = velocity.shape[1]
    rows = velocity.shape[2]
    shells = lax.axis_size("row")
    loop_size = lax.axis_size("theta")
    grid_r = rows * shells
    grid_t = width * loop_size
    shell_index = lax.axis_index("row")
    azimuth_ext = extended(velocity, (("theta", 1),), 2, True)
    radial_ext = extended(velocity, (("row", 2),), 2, False)
    inner_rows = velocity[:, :, :2]
    facing = shifted(inner_rows, "theta", loop_size // 2)
    parity = jnp.array([-1.0, -1.0, 1.0], jnp.float32).reshape(3, 1, 1, 1)
    lower_ghost = jnp.where(shell_index == 0, parity * facing[:, :, ::-1], radial_ext[:, :, :2])
    upper_ghost = jnp.where(
        shell_index == shells - 1,
        -velocity[:, :, rows - 2 :][:, :, ::-1],
        radial_ext[:, :, rows + 2 :],
    )
    radial_ext = jnp.concatenate([lower_ghost, velocity, upper_ghost], axis=2)
    shell_pos = (shell_index * rows + jnp.arange(rows)).astype(jnp.float32).reshape(rows, 1)
    return tendencies(velocity, radial_ext, azimuth_ext, shell_pos, grid_r, grid_t)


def solution(mesh):
    return jax.shard_map(
        per_device,
        mesh=mesh,
        in_specs=(P(None, "theta", "row", None),),
        out_specs=(P(None, "theta", "row", None), P(None, "theta", "row", None)),
        check_vma=False,
    )
```

profile of v0, /device:TPU:1, one launch (start us, length us, event | category | flops | bytes accessed | tf_op | source)
XLA Modules:
  0.0 92.1 jit_solution(16031620928843153056)
XLA Ops:
  0.6 0.0 copy-start
  0.6 1.1 %fusion.27 = (f32[3,8,2,128]{3,2,1,0:T(2,128)S(1)}, f32[3,8,2,128]{3,2,1,0:T(2,128)S(1)}) fusion(f32[3,8,384,128]{3,2,1,0:T(8,128)} %param.2), kind=kLoop, calls=%fused_computation.55 | loop fusion | bytes 98304 | tf_op jit(solution)/shard_map/slice | solution.py:85
  1.8 2.2 %collective-permute-start.1 = (f32[3,8,2,128]{3,2,1,0:T(2,128)S(1)}, f32[3,8,2,128]{3,2,1,0:T(2,128)S(1)}, u32[]{:S(2)}, u32[]{:S(2)}) collective-permute-start(f32[3,8,2,128]{3,2,1,0:T(2,128)S(1)} %get-tuple-element.25), channel_id=1, source_target_pairs={{0,128},{4,132},{8,136},{12,140},{16,144},{20,148},{24,152},{28,15... | collective-permute-start | bytes 73736 | tf_op jit(solution)/shard_map/ppermute | solution.py:28
  4.0 3.2 %collective-permute-start = (f32[3,8,2,128]{3,2,1,0:T(2,128)S(1)}, f32[3,8,2,128]{3,2,1,0:T(2,128)S(1)}, u32[]{:S(2)}, u32[]{:S(2)}) collective-permute-start(f32[3,8,2,128]{3,2,1,0:T(2,128)S(1)} %get-tuple-element.25), channel_id=1, source_target_pairs={{1,0},{2,1},{3,2},{5,4},{6,5},{7,6},{9,8},{10,9},{11,10},{13,12},{... | collective-permute-start | bytes 73736 | tf_op jit(solution)/shard_map/ppermute | solution.py:19
  7.1 4.1 %collective-permute-start.2 = (f32[3,8,2,128]{3,2,1,0:T(2,128)S(1)}, f32[3,8,2,128]{3,2,1,0:T(2,128)S(1)}, u32[]{:S(2)}, u32[]{:S(2)}) collective-permute-start(f32[3,8,2,128]{3,2,1,0:T(2,128)S(1)} %get-tuple-element.26), channel_id=1, source_target_pairs={{0,1},{1,2},{2,3},{4,5},{5,6},{6,7},{8,9},{9,10},{10,11},{12,13},{... | collective-permute-start | bytes 73736 | tf_op jit(solution)/shard_map/ppermute | solution.py:17
  11.3 3.2 %fusion.22 = (f32[3,2,384,128]{3,2,1,0:T(8,128)}, f32[3,2,384,128]{3,2,1,0:T(8,128)}) fusion(f32[3,8,384,128]{3,2,1,0:T(8,128)} %param.2), kind=kLoop, calls=%fused_computation.50 | loop fusion | bytes 4718592 | tf_op jit(solution)/shard_map/slice | solution.py:13
  14.4 7.6 %collective-permute-start.3 = (f32[3,2,384,128]{3,2,1,0:T(8,128)}, f32[3,2,384,128]{3,2,1,0:T(8,128)S(1)}, u32[]{:S(2)}, u32[]{:S(2)}) collective-permute-start(f32[3,2,384,128]{3,2,1,0:T(8,128)} %get-tuple-element.13), channel_id=1, source_target_pairs={{4,0},{8,4},{12,8},{16,12},{20,16},{24,20},{28,24},{32,28},{36,32}... | collective-permute-start | bytes 3538952 | tf_op jit(solution)/shard_map/ppermute | solution.py:19
  22.0 0.0 collective-permute-start.4
  22.0 0.0 copy-done
  22.0 5.4 %fusion.25 = (f32[3,8,384,2]{3,2,1,0:T(8,128)}, f32[3,8,384,2]{3,2,1,0:T(8,128)}) fusion(f32[3,8,384,128]{3,2,1,0:T(8,128)S(1)} %copy-done), kind=kLoop, calls=%fused_computation.53 | loop fusion | bytes 294912 | tf_op jit(solution)/shard_map/jit(_roll_static)/slice | solution.py:57
  27.4 5.2 %fusion.24 = (f32[3,8,384,1]{3,2,1,0:T(8,128)}, f32[3,8,384,1]{3,2,1,0:T(8,128)}) fusion(f32[3,8,384,128]{3,2,1,0:T(8,128)S(1)} %copy-done), kind=kLoop, calls=%fused_computation.52 | loop fusion | bytes 147456 | tf_op jit(solution)/shard_map/jit(_roll_static)/slice | solution.py:54
  32.6 5.4 %fusion.23 = (f32[3,8,384,127]{3,2,1,0:T(8,128)}, f32[3,8,384,127]{3,2,1,0:T(8,128)}) fusion(f32[3,8,384,128]{3,2,1,0:T(8,128)S(1)} %copy-done), kind=kLoop, calls=%fused_computation.51 | loop fusion | bytes 18726912 | tf_op jit(solution)/shard_map/jit(_roll_static)/slice | solution.py:54
  38.0 8.9 %fusion.26 = (f32[3,8,384,126]{3,2,1,0:T(8,128)}, f32[3,8,384,126]{3,2,1,0:T(8,128)}) fusion(f32[3,8,384,128]{3,2,1,0:T(8,128)} %param.2), kind=kLoop, calls=%fused_computation.54 | loop fusion | bytes 18579456 | tf_op jit(solution)/shard_map/jit(_roll_static)/slice | solution.py:57
  46.9 0.1 rev.6
  46.9 0.1 pad.5.clone
  47.0 0.0 collective-permute-done
  47.0 0.0 collective-permute-done.1
  47.0 0.1 rev.7
  47.1 0.0 collective-permute-done.2
  47.1 0.1 multiply_select_fusion
  47.2 5.8 %collective-permute-done.4 = f32[3,2,384,128]{3,2,1,0:T(8,128)S(1)} collective-permute-done((f32[3,2,384,128]{3,2,1,0:T(8,128)}, f32[3,2,384,128]{3,2,1,0:T(8,128)S(1)}, u32[]{:S(2)}, u32[]{:S(2)}) %collective-permute-start.4) | collective-permute-done | bytes 1179680 | tf_op jit(solution)/shard_map/ppermute | solution.py:17
  53.0 0.1 constant_dynamic-update-slice_fusion.3
  53.0 3.4 %constant_dynamic-update-slice_fusion.1 = (f32[3,10,384,128]{3,2,1,0:T(8,128)S(1)}, f32[3,10,384,128]{3,2,1,0:T(8,128)S(1)}) fusion(f32[3,8,384,128]{3,2,1,0:T(8,128)} %param.2, f32[3,10,384,128]{3,2,1,0:T(8,128)S(1)} %constant_dynamic-update-slice_fusion.3), kind=kLoop, calls=%fused_computation.42 | loop fusion | bytes 14155776
  56.5 0.0 collective-permute-done.3
  56.5 0.0 slice-start
  56.5 0.1 constant_dynamic-update-slice_fusion
  56.6 0.0 slice-start.1
  56.6 4.4 %broadcast_multiply_fusion = (f32[3,8,384,128]{3,2,1,0:T(8,128)}, f32[3,8,384,128]{3,2,1,0:T(8,128)}) fusion(f32[3,10,384,128]{3,2,1,0:T(8,128)S(1)} %get-tuple-element.16, f32[3,10,384,128]{3,2,1,0:T(8,128)S(1)} %constant_dynamic-update-slice_fusion), kind=kLoop, calls=%fused_computation.30 | loop fusion | flops 5898240 | bytes 28311552 | tf_op jit(solution)/shard_map/div | solution.py:47
  61.0 0.0 slice-done.1
  61.0 7.2 %multiply_bitcast_fusion = (f32[8,384,128]{2,1,0:T(8,128)}, f32[1,8,384,128]{3,2,1,0:T(8,128)}, f32[1,8,384,128]{3,2,1,0:T(8,128)}, f32[1,8,384,128]{3,2,1,0:T(8...) fusion(f32[3,8,384,128]{3,2,1,0:T(8,128)S(1)} %bitcast.11, ...), kind=kLoop, calls=%fused_computation.36 | loop fusion | flops 5505024 | bytes 18877440 | tf_op jit(solution)/shard_map/mul | solution.py:70
  68.2 7.2 %fusion.15 = bf16[3,8,384,128]{3,2,1,0:T(8,128)(2,1)} fusion(f32[1,8,384,128]{3,2,1,0:T(8,128)} %get-tuple-element.7, f32[1,8,384,128]{3,2,1,0:T(8,128)} %get-tuple-element.8, f32[1,8,384,128]{3,2,1,0:T(8,128)} %get-tuple-element.9, f32[1,8,384,128]{3,2,1,0:T(8,128)} %get-tuple-element.10, f32[3,8,384,128]{3,2,1,0:T(8,128)} %get-tuple-element.3, ...), kind=kLoop, calls=%fused_computation.26 | loop fusion | flops 17694720 | bytes 29097996 | tf_op jit(solution)/shard_map/convert_element_type | solution.py:72
  75.4 16.7 %fusion.10 = bf16[3,8,384,128]{3,2,1,0:T(8,128)(2,1)} fusion(f32[3,8,384,128]{3,2,1,0:T(8,128)S(1)} %bitcast.11, f32[3,8,2,128]{3,2,1,0:T(2,128)S(1)} %multiply_select_fusion, f32[3,8,2,128]{3,2,1,0:T(2,128)S(1)} %bitcast.13, f32[3,8,384,2]{3,2,1,0:T(8,128)} %get-tuple-element.22, f32[3,8,384,126]{3,2,1,0:T(8,128)} %get-tuple-element.24, ...), kind=kLoop, calls=%fused_computation.16 | loop fusion | flops 41287680 | bytes 29151744 | tf_op jit(solution)/shard_map/convert_element_type | solution.py:72
  (12 shorter events, 0.0 us)
Async XLA Ops:
  0.6 21.4 %copy-start = (f32[3,8,384,128]{3,2,1,0:T(8,128)S(1)}, f32[3,8,384,128]{3,2,1,0:T(8,128)}, u32[]{:S(2)}) copy-start(f32[3,8,384,128]{3,2,1,0:T(8,128)} %param.2) | copy-start | bytes 14155780
  1.8 45.3 %collective-permute-start.1 = (f32[3,8,2,128]{3,2,1,0:T(2,128)S(1)}, f32[3,8,2,128]{3,2,1,0:T(2,128)S(1)}, u32[]{:S(2)}, u32[]{:S(2)}) collective-permute-start(f32[3,8,2,128]{3,2,1,0:T(2,128)S(1)} %get-tuple-element.25), channel_id=1, source_target_pairs={{0,128},{4,132},{8,136},{12,140},{16,144},{20,148},{24,152},{28,15... | collective-permute-start | bytes 73736 | tf_op jit(solution)/shard_map/ppermute | solution.py:28
  4.0 43.0 %collective-permute-start = (f32[3,8,2,128]{3,2,1,0:T(2,128)S(1)}, f32[3,8,2,128]{3,2,1,0:T(2,128)S(1)}, u32[]{:S(2)}, u32[]{:S(2)}) collective-permute-start(f32[3,8,2,128]{3,2,1,0:T(2,128)S(1)} %get-tuple-element.25), channel_id=1, source_target_pairs={{1,0},{2,1},{3,2},{5,4},{6,5},{7,6},{9,8},{10,9},{11,10},{13,12},{... | collective-permute-start | bytes 73736 | tf_op jit(solution)/shard_map/ppermute | solution.py:19
  7.1 39.9 %collective-permute-start.2 = (f32[3,8,2,128]{3,2,1,0:T(2,128)S(1)}, f32[3,8,2,128]{3,2,1,0:T(2,128)S(1)}, u32[]{:S(2)}, u32[]{:S(2)}) collective-permute-start(f32[3,8,2,128]{3,2,1,0:T(2,128)S(1)} %get-tuple-element.26), channel_id=1, source_target_pairs={{0,1},{1,2},{2,3},{4,5},{5,6},{6,7},{8,9},{9,10},{10,11},{12,13},{... | collective-permute-start | bytes 73736 | tf_op jit(solution)/shard_map/ppermute | solution.py:17
  14.4 42.0 %collective-permute-start.3 = (f32[3,2,384,128]{3,2,1,0:T(8,128)}, f32[3,2,384,128]{3,2,1,0:T(8,128)S(1)}, u32[]{:S(2)}, u32[]{:S(2)}) collective-permute-start(f32[3,2,384,128]{3,2,1,0:T(8,128)} %get-tuple-element.13), channel_id=1, source_target_pairs={{4,0},{8,4},{12,8},{16,12},{20,16},{24,20},{28,24},{32,28},{36,32}... | collective-permute-start | bytes 3538952 | tf_op jit(solution)/shard_map/ppermute | solution.py:19
  22.0 30.9 %collective-permute-start.4 = (f32[3,2,384,128]{3,2,1,0:T(8,128)}, f32[3,2,384,128]{3,2,1,0:T(8,128)S(1)}, u32[]{:S(2)}, u32[]{:S(2)}) collective-permute-start(f32[3,2,384,128]{3,2,1,0:T(8,128)} %get-tuple-element.14), channel_id=1, source_target_pairs={{0,4},{4,8},{8,12},{12,16},{16,20},{20,24},{24,28},{28,32},{32,36}... | collective-permute-start | bytes 3538952 | tf_op jit(solution)/shard_map/ppermute | solution.py:17
  38.0 9.1 %copy-start.3 = (f32[3]{0:T(128)S(1)}, f32[3]{0:T(128)}, u32[]{:S(2)}) copy-start(f32[3]{0:T(128)} %constant.48.clone) | copy-start | bytes 40
  56.5 4.5 %slice-start = ((s8[4718592]{0:T(1024)(128)(4,1)}), s8[4194304]{0:T(1024)(128)(4,1)S(1)}, s32[]{:S(2)}) async-start(s8[4718592]{0:T(1024)(128)(4,1)} %bitcast.10), calls=%async_computation | async-start | bytes 8388608
  56.6 4.4 %slice-start.1 = ((s8[4718592]{0:T(1024)(128)(4,1)}), s8[524288]{0:T(1024)(128)(4,1)S(1)}, s32[]{:S(2)}) async-start(s8[4718592]{0:T(1024)(128)(4,1)} %bitcast.10), calls=%async_computation.1 | async-start | bytes 1048576
  68.2 7.2 %copy-start.1 = (f32[8,384,128]{2,1,0:T(8,128)S(1)}, f32[8,384,128]{2,1,0:T(8,128)}, u32[]{:S(2)}) copy-start(f32[8,384,128]{2,1,0:T(8,128)} %get-tuple-element.11) | copy-start | bytes 4718596
  68.2 7.2 %copy-start.2 = (f32[8,384,128]{2,1,0:T(8,128)S(1)}, f32[8,384,128]{2,1,0:T(8,128)}, u32[]{:S(2)}) copy-start(f32[8,384,128]{2,1,0:T(8,128)} %get-tuple-element.12) | copy-start | bytes 4718596
where the time goes:
time: 92.3 us; the launch traced here: 92.1 us
  other arithmetic  35.6 us (39%)
  local copies, waits for them, and re-layouts  32.9 us (36%)
  starting transfers between devices  17.1 us (19%)
  waiting for transfers between devices  5.79 us (6%)
    convert_element_type x1, other arithmetic, tendencies(): radial_part.astype(jnp.bfloat16)  16.7 us
    slice x2, local copies, waits for them, and re-layouts, tendencies(): behind_two = jnp.roll(velocity, 2, axis=3)  14.2 us
    ppermute x2, starting transfers between devices, extended(): lax.ppermute(head, axis, [((i + 1) % count, i) for i in range(ends)])  10.7 us
    slice x2, local copies, waits for them, and re-layouts, tendencies(): ahead_one = jnp.roll(velocity, -1, axis=3)  10.6 us
    mul x1, other arithmetic, tendencies(): -radius * u_ang * angle_slope + curvature + viscosity * (angle_lap + metric)  7.21 us
    convert_element_type x1, other arithmetic, tendencies(): azimuthal_part.astype(jnp.bfloat16)  7.17 us
    ppermute x2, waiting for transfers between devices, extended(): lax.ppermute(tail, axis, [(i, (i + 1) % count) for i in range(ends)])  5.78 us
    div x1, other arithmetic, tendencies(): (8.0 * (azimuth_ext[:, 3:-1] - azimuth_ext[:, 1:-3]) - (azimuth_ext[:, 4:...  4.41 us
  transfers between devices with their start and end apart: 5, of which 1 were waited for; matrix products, arithmetic and copies ran while one was open for 35% of the time, Pallas kernels for 0%

commit v1 on v0

v1 whole, which is shorter than its diff:
```python
import functools
import math

import jax
import jax.numpy as jnp
from jax import lax
from jax.experimental import pallas as pl
from jax.experimental.pallas import tpu as pltpu
from jax.sharding import PartitionSpec as P

MESH = pl.DeviceIdType.MESH
PAD = 8
BLOCK = 32
PIECES = 4


def radial_block(ext, weights, out, m, row, grid_r):
    slope_r = 0.2 / 12.0
    slope_z = 0.2 / 48.0
    lap_r = 0.1
    lap_z = 0.1 / 16.0
    mid = pl.ds(row + PAD, BLOCK)
    inverse = weights[0, pl.ds(row, BLOCK), :]
    u_rad = ext[0, m + 2, mid, :]
    u_ax = ext[2, m + 2, mid, :]
    radial_two = u_rad * (-slope_r)
    radial_one = radial_two * 8.0 + lap_r * inverse
    axial_two = u_ax * (-slope_z)
    axial_one = axial_two * 8.0
    for c in range(3):
        f = ext[c, m + 2, mid, :]
        out_one = ext[c, m + 2, pl.ds(row + PAD + 1, BLOCK), :]
        in_one = ext[c, m + 2, pl.ds(row + PAD - 1, BLOCK), :]
        out_two = ext[c, m + 2, pl.ds(row + PAD + 2, BLOCK), :]
        in_two = ext[c, m + 2, pl.ds(row + PAD - 2, BLOCK), :]
        planes = f.shape[1]
        ahead_one = pltpu.roll(f, planes - 1, 1)
        behind_one = pltpu.roll(f, 1, 1)
        ahead_two = pltpu.roll(f, planes - 2, 1)
        behind_two = pltpu.roll(f, 2, 1)
        total = (out_one - in_one) * radial_one - (out_two - in_two) * radial_two
        total += (ahead_one - behind_one) * axial_one - (ahead_two - behind_two) * axial_two
        total += (out_one + in_one) * lap_r + (ahead_one + behind_one) * lap_z
        total -= f * (2.0 * (lap_r + lap_z))
        out[c, m, pl.ds(row, BLOCK), :] = total.astype(out.dtype)


def azimuth_block(ext, weights, out, m, row, grid_r, grid_t):
    step = 2.0 * math.pi / grid_t
    angle_time = 2.0 / grid_r
    small = angle_time * 0.5 / grid_r
    lap = small / (step * step)
    slope = 8.0 / (12.0 * step)
    mid = pl.ds(row + PAD, BLOCK)
    radius = weights[1, pl.ds(row, BLOCK), :] * angle_time
    u_rad = ext[0, m + 2, mid, :]
    u_ang = ext[1, m + 2, mid, :]
    carried = radius * u_ang
    slopes, totals = [], []
    for c in range(3):
        f = u_rad if c == 0 else u_ang if c == 1 else ext[c, m + 2, mid, :]
        up = ext[c, m + 3, mid, :]
        down = ext[c, m + 1, mid, :]
        wide = ext[c, m + 4, mid, :] - ext[c, m, mid, :]
        slopes.append(((up - down) - wide * 0.125) * slope)
        totals.append((up + down) * lap - f * (2.0 * lap if c == 2 else 2.0 * lap + small))
    totals[0] += carried * (u_ang - slopes[0]) - slopes[1] * (2.0 * small)
    totals[1] += slopes[0] * (2.0 * small) - carried * (u_rad + slopes[1])
    totals[2] -= carried * slopes[2]
    for c in range(3):
        out[c, m, pl.ds(row, BLOCK), :] = totals[c].astype(out.dtype)


def tendencies(loop_size, shells, v, radial, azimuth, ext, weights, own_sem, send_sem, recv_sem, ghost_send, ghost_recv):
    width, rows = v.shape[1], v.shape[2]
    grid_r, grid_t = rows * shells, width * loop_size
    top = rows + PAD
    t = lax.axis_index("theta")
    shell = lax.axis_index("row")
    right, left = lax.rem(t + 1, loop_size), lax.rem(t + loop_size - 1, loop_size)
    opposite = lax.rem(t + loop_size // 2, loop_size)
    innermost, outermost = shell == 0, shell == shells - 1
    inner = lax.max(shell - 1, 0)
    outer = lax.min(shell + 1, shells - 1)

    def signal(barrier, at):
        pl.semaphore_signal(barrier, inc=1, device_id=at, device_id_type=MESH)

    barrier = pltpu.get_barrier_semaphore()
    signal(barrier, (right, shell))
    signal(barrier, (left, shell))
    pl.when(innermost)(lambda: signal(barrier, (opposite, shell)))
    pl.when(jnp.logical_not(innermost))(lambda: signal(barrier, (t, inner)))
    pl.when(jnp.logical_not(outermost))(lambda: signal(barrier, (t, outer)))

    own = pltpu.make_async_copy(v, ext.at[:, pl.ds(2, width), pl.ds(PAD, rows), :], own_sem)
    own.start()

    pl.semaphore_wait(barrier, jnp.where(outermost, 3, 4))

    size = rows // PIECES
    arriving = []
    for p in range(PIECES):
        part, there = pl.ds(p * size, size), pl.ds(PAD + p * size, size)
        for d, (at, src, dst) in enumerate(((right, width - 2, 0), (left, 0, width + 2))):
            copy = pltpu.make_async_remote_copy(
                src_ref=v.at[:, pl.ds(src, 2), part, :],
                dst_ref=ext.at[:, pl.ds(dst, 2), there, :],
                send_sem=send_sem.at[d, p],
                recv_sem=recv_sem.at[d, p],
                device_id=(at, shell),
                device_id_type=MESH,
            )
            copy.start()
            arriving.append(copy)
        if p == 0:
            layers = pl.ds(2, width)
            inward = pltpu.make_async_remote_copy(
                src_ref=v.at[:, :, pl.ds(0, PAD), :],
                dst_ref=ext.at[:, layers, pl.ds(top, PAD), :],
                send_sem=ghost_send.at[0],
                recv_sem=ghost_recv.at[0],
                device_id=(t, inner),
                device_id_type=MESH,
            )
            across = pltpu.make_async_remote_copy(
                src_ref=v.at[:, :, pl.ds(0, PAD), :],
                dst_ref=ext.at[:, layers, pl.ds(0, PAD), :],
                send_sem=ghost_send.at[0],
                recv_sem=ghost_recv.at[1],
                device_id=(opposite, shell),
                device_id_type=MESH,
            )
            outward = pltpu.make_async_remote_copy(
                src_ref=v.at[:, :, pl.ds(rows - PAD, PAD), :],
                dst_ref=ext.at[:, layers, pl.ds(0, PAD), :],
                send_sem=ghost_send.at[1],
                recv_sem=ghost_recv.at[1],
                device_id=(t, outer),
                device_id_type=MESH,
            )
            pl.when(innermost)(across.start)
            pl.when(jnp.logical_not(innermost))(inward.start)
            pl.when(jnp.logical_not(outermost))(outward.start)

    blocks = rows // BLOCK

    @pl.loop(0, blocks)
    def _(b):
        row = pl.multiple_of(b * BLOCK, BLOCK)
        place = lax.broadcasted_iota(jnp.int32, (BLOCK, v.shape[3]), 0) + (shell * rows + row)
        place = place.astype(jnp.float32)
        weights[0, pl.ds(row, BLOCK), :] = 1.0 / (2.0 * place + 1.0)
        weights[1, pl.ds(row, BLOCK), :] = (place + 0.5) * (1.0 / grid_r)

    own.wait()

    @pl.loop(0, blocks)
    def _(b):
        row = pl.multiple_of(b * BLOCK, BLOCK)
        for m in range(2, width - 2):
            azimuth_block(ext, weights, azimuth, m, row, grid_r, grid_t)

    across.wait_recv()
    pl.when(jnp.logical_not(outermost))(inward.wait_recv)

    @pl.when(innermost)
    def _():
        for c, sign in enumerate((-1.0, -1.0, 1.0)):
            for m in range(2, width + 2):
                facing = ext[c, m, 0:PAD, :]
                ext[c, m, PAD - 1 : PAD, :] = facing[0:1] * sign
                ext[c, m, PAD - 2 : PAD - 1, :] = facing[1:2] * sign

    @pl.when(outermost)
    def _():
        for c in range(3):
            for m in range(2, width + 2):
                last = ext[c, m, top - PAD : top, :]
                ext[c, m, top : top + 1, :] = -last[PAD - 1 : PAD]
                ext[c, m, top + 1 : top + 2, :] = -last[PAD - 2 : PAD - 1]

    @pl.loop(0, blocks)
    def _(b):
        row = pl.multiple_of(b * BLOCK, BLOCK)

        @pl.loop(0, width)
        def _(m):
            radial_block(ext, weights, radial, m, row, grid_r)

    for p in range(PIECES):
        for d in range(2):
            arriving[2 * p + d].wait_recv()

        @pl.loop(p * (size // BLOCK), (p + 1) * (size // BLOCK))
        def _(b):
            row = pl.multiple_of(b * BLOCK, BLOCK)
            for m in (0, 1, width - 2, width - 1):
                azimuth_block(ext, weights, azimuth, m, row, grid_r, grid_t)

    for copy in arriving:
        copy.wait_send()
    inward.wait_send()
    pl.when(jnp.logical_not(outermost))(outward.wait_send)


def write_out(radial_in, azimuth_in, radial, azimuth, sems):
    copies = []
    for k, (src, dst) in enumerate(((radial_in, radial), (azimuth_in, azimuth))):
        for c in range(3):
            copies.append(pltpu.make_async_copy(src.at[c], dst.at[c], sems.at[k, c]))
    for copy in copies:
        copy.start()
    for copy in copies:
        copy.wait()


def solution(mesh):
    loop_size, shells = mesh.shape["theta"], mesh.shape["row"]

    def per_device(v):
        _, width, rows, planes = v.shape
        result = jax.ShapeDtypeStruct(v.shape, jnp.bfloat16)
        held = pltpu.VMEM(v.shape, jnp.bfloat16)
        vmem = pl.BlockSpec(memory_space=pltpu.VMEM)
        hbm = pl.BlockSpec(memory_space=pltpu.HBM)
        dma = pltpu.SemaphoreType.DMA
        radial, azimuth = pl.pallas_call(
            functools.partial(tendencies, loop_size, shells),
            out_shape=(held, held),
            in_specs=[hbm],
            out_specs=(vmem, vmem),
            scratch_shapes=[
                pltpu.VMEM((3, width + 4, rows + 2 * PAD, planes), jnp.float32),
                pltpu.VMEM((2, rows, planes), jnp.float32),
                dma,
                dma((2, PIECES)),
                dma((2, PIECES)),
                dma((2,)),
                dma((2,)),
            ],
            compiler_params=pltpu.CompilerParams(
                collective_id=0, has_side_effects=True, vmem_limit_bytes=32 << 20
            ),
        )(pltpu.with_memory_space_constraint(v, pltpu.HBM))
        radial = pltpu.with_memory_space_constraint(radial, pltpu.VMEM)
        azimuth = pltpu.with_memory_space_constraint(azimuth, pltpu.VMEM)
        return pl.pallas_call(
            write_out,
            out_shape=(result, result),
            in_specs=[vmem, vmem],
            out_specs=(hbm, hbm),
            scratch_shapes=[dma((2, 3))],
            compiler_params=pltpu.CompilerParams(vmem_limit_bytes=32 << 20),
        )(radial, azimuth)

    spec = P(None, "theta", "row", None)
    return jax.shard_map(
        per_device, mesh=mesh, in_specs=(spec,), out_specs=(spec, spec), check_vma=False
    )
```

time: 92.3 us -> 55.9 us (0.61)
  Pallas kernels: 0 us -> 55.2 us
  other arithmetic: 35.6 us -> 0 us
  local copies, waits for them, and re-layouts: 32.9 us -> 0 us
  starting transfers between devices: 17.1 us -> 0 us
  waiting for transfers between devices: 5.79 us -> 0 us
    pallas_call x0 -> x2, Pallas kernels: none -> 55.2 us  [the longest x1 52.9 us: per_device(): pl.pallas_call(functools.partial(tendencies, loop_size, shells), out_shap...]
    slice x6 -> x0, local copies, waits for them, and re-layouts: 29.1 us -> none  [the longest x2 14.2 us: tendencies(): behind_two = jnp.roll(velocity, 2, axis=3)]
    convert_element_type x3 -> x0, other arithmetic: 23.9 us -> none  [the longest x1 16.7 us: tendencies(): radial_part.astype(jnp.bfloat16)]
    ppermute x5 -> x0, starting transfers between devices: 17.1 us -> none  [the longest x2 10.7 us: extended(): lax.ppermute(head, axis, [((i + 1) % count, i) for i in range(ends)])]
    mul x3 -> x0, other arithmetic: 7.22 us -> none  [the longest x1 7.21 us: tendencies(): -radius * u_ang * angle_slope + curvature + viscosity * (angle_lap + metric)]
    ppermute x5 -> x0, waiting for transfers between devices: 5.79 us -> none  [the longest x2 5.78 us: extended(): lax.ppermute(tail, axis, [(i, (i + 1) % count) for i in range(ends)])]
    div x1 -> x0, other arithmetic: 4.41 us -> none  [tendencies(): (8.0 * (azimuth_ext[:, 3:-1] - azimuth_ext[:, 1:-3]) - (azimuth_ext[:, 4:...]
    unnamed x14 -> x0, local copies, waits for them, and re-layouts: 3.55 us -> none
  transfers between devices with their start and end apart: 5 -> 0, of which waited for: 1 -> 0; matrix products, arithmetic and copies ran while one was open for 35% -> 0% of each run, Pallas kernels for 0% -> 0%
where the time goes in v1:
time: 55.9 us; the launch traced here: 55.8 us
  Pallas kernels  55.2 us (99%)
  between operations  0.64 us (1%)
    pallas_call x1, Pallas kernels, per_device(): pl.pallas_call(functools.partial(tendencies, loop_size, shells), out_shap...  52.9 us
    pallas_call x1, Pallas kernels, per_device(): pl.pallas_call(write_out, out_shape=(result, result), in_specs=[vmem, vme...  2.23 us

profile of v1, /device:TPU:1, one launch (start us, length us, event | category | flops | bytes accessed | tf_op | source)
XLA Modules:
  0.0 55.8 jit_solution(14193605917314936952)
XLA Ops:
  0.6 52.9 %shard_map.30 = (bf16[3,8,384,128]{3,2,1,0:T(8,128)(2,1)S(1)}, bf16[3,8,384,128]{3,2,1,0:T(8,128)(2,1)S(1)}) custom-call(f32[3,8,384,128]{3,2,1,0:T(8,128)} %v.1), custom_call_target="tpu_custom_call" | custom-call | tf_op jit(solution)/shard_map/pallas_call | solution.py:228
  53.6 2.2 %shard_map.31 = (bf16[3,8,384,128]{3,2,1,0:T(8,128)(2,1)}, bf16[3,8,384,128]{3,2,1,0:T(8,128)(2,1)}) custom-call(bf16[3,8,384,128]{3,2,1,0:T(8,128)(2,1)S(1)} %get-tuple-element.4.radial_in, bf16[3,8,384,128]{3,2,1,0:T(8,128)(2,1)S(1)} %get-tuple-element.5.azimuth_in), custom_call_target="tpu_custom_call" | custom-call | tf_op jit(solution)/shard_map/pallas_call | solution.py:248

commit v2 on v1

v2 whole, which is shorter than its diff:
```python
import functools
import math

import jax
import jax.numpy as jnp
from jax import lax
from jax.experimental import pallas as pl
from jax.experimental.pallas import tpu as pltpu
from jax.sharding import PartitionSpec as P

MESH = pl.DeviceIdType.MESH
PAD = 8
BLOCK = 32
RUN = 8
END = 16
PIECES = 4


def radial_block(ext, weights, out, m, row, count):
    slope_r = 0.2 / 12.0
    slope_z = 0.2 / 48.0
    lap_r = 0.1
    lap_z = 0.1 / 16.0
    mid = pl.ds(row + PAD, count)
    inverse = weights[0, pl.ds(row, count), :]
    u_rad = ext[0, m + 2, mid, :]
    u_ax = ext[2, m + 2, mid, :]
    radial_two = u_rad * (-slope_r)
    radial_one = radial_two * 8.0 + lap_r * inverse
    axial_two = u_ax * (-slope_z)
    axial_one = axial_two * 8.0
    for c in range(3):
        f = ext[c, m + 2, mid, :]
        out_one = ext[c, m + 2, pl.ds(row + PAD + 1, count), :]
        in_one = ext[c, m + 2, pl.ds(row + PAD - 1, count), :]
        out_two = ext[c, m + 2, pl.ds(row + PAD + 2, count), :]
        in_two = ext[c, m + 2, pl.ds(row + PAD - 2, count), :]
        planes = f.shape[1]
        ahead_one = pltpu.roll(f, planes - 1, 1)
        behind_one = pltpu.roll(f, 1, 1)
        ahead_two = pltpu.roll(f, planes - 2, 1)
        behind_two = pltpu.roll(f, 2, 1)
        total = (out_one - in_one) * radial_one - (out_two - in_two) * radial_two
        total += (ahead_one - behind_one) * axial_one - (ahead_two - behind_two) * axial_two
        total += (out_one + in_one) * lap_r + (ahead_one + behind_one) * lap_z
        total -= f * (2.0 * (lap_r + lap_z))
        out[c, m, pl.ds(row, count), :] = total.astype(out.dtype)


def azimuth_block(ext, weights, out, m, row, grid_r, grid_t):
    step = 2.0 * math.pi / grid_t
    angle_time = 2.0 / grid_r
    small = angle_time * 0.5 / grid_r
    lap = small / (step * step)
    slope = 8.0 / (12.0 * step)
    mid = pl.ds(row + PAD, BLOCK)
    radius = weights[1, pl.ds(row, BLOCK), :] * angle_time
    u_rad = ext[0, m + 2, mid, :]
    u_ang = ext[1, m + 2, mid, :]
    carried = radius * u_ang
    slopes, totals = [], []
    for c in range(3):
        f = u_rad if c == 0 else u_ang if c == 1 else ext[c, m + 2, mid, :]
        up = ext[c, m + 3, mid, :]
        down = ext[c, m + 1, mid, :]
        wide = ext[c, m + 4, mid, :] - ext[c, m, mid, :]
        slopes.append(((up - down) - wide * 0.125) * slope)
        totals.append((up + down) * lap - f * (2.0 * lap if c == 2 else 2.0 * lap + small))
    totals[0] += carried * (u_ang - slopes[0]) - slopes[1] * (2.0 * small)
    totals[1] += slopes[0] * (2.0 * small) - carried * (u_rad + slopes[1])
    totals[2] -= carried * slopes[2]
    for c in range(3):
        out[c, m, pl.ds(row, BLOCK), :] = totals[c].astype(out.dtype)


def tendencies(
    loop_size, shells, v, radial, azimuth, ext, weights, stage, ghost,
    own_sem, send_sem, recv_sem, ghost_send, ghost_recv, ready, turn,
):
    width, rows = v.shape[1], v.shape[2]
    grid_r, grid_t = rows * shells, width * loop_size
    top = rows + PAD
    t = lax.axis_index("theta")
    shell = lax.axis_index("row")
    right, left = lax.rem(t + 1, loop_size), lax.rem(t + loop_size - 1, loop_size)
    opposite = lax.rem(t + loop_size // 2, loop_size)
    innermost, outermost = shell == 0, shell == shells - 1
    not_innermost, not_outermost = shell > 0, shell < shells - 1
    first_half = innermost & (t < loop_size // 2)
    second_half = innermost & (t >= loop_size // 2)
    inner = lax.max(shell - 1, 0)
    outer = lax.min(shell + 1, shells - 1)

    def signal(sem, at):
        pl.semaphore_signal(sem, inc=1, device_id=at, device_id_type=MESH)

    barrier = pltpu.get_barrier_semaphore()
    signal(barrier, (left, shell))
    pl.when(not_outermost)(lambda: signal(barrier, (t, outer)))
    pl.when(first_half)(lambda: signal(barrier, (opposite, shell)))

    own = pltpu.make_async_copy(v, ext.at[:, pl.ds(2, width), pl.ds(PAD, rows), :], own_sem)
    own.start()

    partners = 1 + not_innermost.astype(jnp.int32) + second_half.astype(jnp.int32)
    pl.semaphore_wait(barrier, partners)
    signal(ready.at[0], (right, shell))
    pl.when(not_innermost)(lambda: signal(ready.at[1], (t, inner)))
    pl.when(second_half)(lambda: signal(ready.at[2], (opposite, shell)))

    size = rows // PIECES

    def layers_copy(d, p):
        at, src, dst = ((right, width - 2, 0), (left, 0, width + 2))[d]
        return pltpu.make_async_remote_copy(
            src_ref=v.at[:, pl.ds(src, 2), pl.ds(p * size, size), :],
            dst_ref=ext.at[:, pl.ds(dst, 2), pl.ds(PAD + p * size, size), :],
            send_sem=send_sem.at[d, p],
            recv_sem=recv_sem.at[d, p],
            device_id=(at, shell),
            device_id_type=MESH,
        )

    rightward = [layers_copy(0, p) for p in range(PIECES)]
    leftward = [layers_copy(1, p) for p in range(PIECES)]

    last_plane = lax.rem(t, RUN) == RUN - 1
    even = lax.rem(shell, 2) == 0
    waits_turn = last_plane & even
    gives_turn = last_plane & jnp.logical_not(even)

    @pl.when(jnp.logical_not(waits_turn))
    def _():
        for copy in rightward:
            copy.start()

    pl.semaphore_wait(ready.at[0], 1)
    for copy in leftward:
        copy.start()

    own.wait()

    for c in range(3):
        for m in range(width):
            at = 2 * (c * width + m)
            head = ext[c, m + 2, PAD : PAD + 2, :]
            across = jnp.concatenate([head[1:2], head[0:1]], axis=0) * (1.0 if c == 2 else -1.0)
            stage[0, at : at + 2, :] = jnp.where(innermost, across, head)
            stage[1, at : at + 2, :] = ext[c, m + 2, top - 2 : top, :]

    def ghost_copy(src, dst, at):
        return pltpu.make_async_remote_copy(
            src_ref=stage.at[src],
            dst_ref=ghost.at[dst],
            send_sem=ghost_send.at[src],
            recv_sem=ghost_recv.at[dst],
            device_id=at,
            device_id_type=MESH,
        )

    across = ghost_copy(0, 0, (opposite, shell))
    inward = ghost_copy(0, 1, (t, inner))
    outward = ghost_copy(1, 0, (t, outer))
    pl.when(not_innermost)(inward.start)

    @pl.when(not_outermost)
    def _():
        pl.semaphore_wait(ready.at[1], 1)
        outward.start()

    pl.when(first_half)(lambda: pl.semaphore_wait(ready.at[2], 1))
    pl.when(innermost)(across.start)

    blocks = rows // BLOCK

    @pl.loop(0, blocks)
    def _(b):
        row = pl.multiple_of(b * BLOCK, BLOCK)
        place = lax.broadcasted_iota(jnp.int32, (BLOCK, v.shape[3]), 0) + (shell * rows + row)
        place = place.astype(jnp.float32)
        weights[0, pl.ds(row, BLOCK), :] = 1.0 / (2.0 * place + 1.0)
        weights[1, pl.ds(row, BLOCK), :] = (place + 0.5) * (1.0 / grid_r)

    @pl.loop(0, blocks)
    def _(b):
        row = pl.multiple_of(b * BLOCK, BLOCK)
        for m in range(2, width - 2):
            azimuth_block(ext, weights, azimuth, m, row, grid_r, grid_t)

    half = rows // 2 - END

    @pl.loop(0, width)
    def _(m):
        radial_block(ext, weights, radial, m, END, half)
        radial_block(ext, weights, radial, m, END + half, half)

    @pl.when(gives_turn)
    def _():
        for copy in rightward:
            copy.wait_send()
        signal(turn, (t, inner))

    @pl.when(waits_turn)
    def _():
        pl.semaphore_wait(turn, 1)
        for copy in rightward:
            copy.start()

    def edge_piece(copy, m, p):
        copy.wait_recv()

        @pl.loop(p * (size // BLOCK), (p + 1) * (size // BLOCK))
        def _(b):
            row = pl.multiple_of(b * BLOCK, BLOCK)
            azimuth_block(ext, weights, azimuth, m, row, grid_r, grid_t)
            azimuth_block(ext, weights, azimuth, m + 1, row, grid_r, grid_t)

    for p in range(PIECES):
        edge_piece(leftward[p], width - 2, p)

    across.wait_recv()
    pl.when(not_outermost)(inward.wait_recv)
    for c in range(3):
        for m in range(width):
            at = 2 * (c * width + m)
            ext[c, m + 2, PAD - 2 : PAD, :] = ghost[0, at : at + 2, :]
            last = ext[c, m + 2, top - 2 : top, :]
            wall = jnp.concatenate([last[1:2], last[0:1]], axis=0) * -1.0
            ext[c, m + 2, top : top + 2, :] = jnp.where(outermost, wall, ghost[1, at : at + 2, :])

    @pl.loop(0, width // 2)
    def _(k):
        for m in (2 * k, 2 * k + 1):
            radial_block(ext, weights, radial, m, 0, END)
            radial_block(ext, weights, radial, m, rows - END, END)

    for p in range(PIECES):
        edge_piece(rightward[p], 0, p)

    for copy in leftward:
        copy.wait_send()

    @pl.when(jnp.logical_not(gives_turn))
    def _():
        for copy in rightward:
            copy.wait_send()

    inward.wait_send()
    pl.when(not_outermost)(outward.wait_send)


def write_out(radial_in, azimuth_in, radial, azimuth, sems):
    copies = []
    for k, (src, dst) in enumerate(((radial_in, radial), (azimuth_in, azimuth))):
        for c in range(3):
            copies.append(pltpu.make_async_copy(src.at[c], dst.at[c], sems.at[k, c]))
    for copy in copies:
        copy.start()
    for copy in copies:
        copy.wait()


def solution(mesh):
    loop_size, shells = mesh.shape["theta"], mesh.shape["row"]

    def per_device(v):
        _, width, rows, planes = v.shape
        result = jax.ShapeDtypeStruct(v.shape, jnp.bfloat16)
        held = pltpu.VMEM(v.shape, jnp.bfloat16)
        vmem = pl.BlockSpec(memory_space=pltpu.VMEM)
        hbm = pl.BlockSpec(memory_space=pltpu.HBM)
        dma = pltpu.SemaphoreType.DMA
        radial, azimuth = pl.pallas_call(
            functools.partial(tendencies, loop_size, shells),
            out_shape=(held, held),
            in_specs=[hbm],
            out_specs=(vmem, vmem),
            scratch_shapes=[
                pltpu.VMEM((3, width + 4, rows + 2 * PAD, planes), jnp.float32),
                pltpu.VMEM((2, rows, planes), jnp.float32),
                pltpu.VMEM((2, 6 * width, planes), jnp.float32),
                pltpu.VMEM((2, 6 * width, planes), jnp.float32),
                dma,
                dma((2, PIECES)),
                dma((2, PIECES)),
                dma((2,)),
                dma((2,)),
                pltpu.SemaphoreType.REGULAR((3,)),
                pltpu.SemaphoreType.REGULAR,
            ],
            compiler_params=pltpu.CompilerParams(
                collective_id=0, has_side_effects=True, vmem_limit_bytes=32 << 20
            ),
        )(pltpu.with_memory_space_constraint(v, pltpu.HBM))
        radial = pltpu.with_memory_space_constraint(radial, pltpu.VMEM)
        azimuth = pltpu.with_memory_space_constraint(azimuth, pltpu.VMEM)
        return pl.pallas_call(
            write_out,
            out_shape=(result, result),
            in_specs=[vmem, vmem],
            out_specs=(hbm, hbm),
            scratch_shapes=[dma((2, 3))],
            compiler_params=pltpu.CompilerParams(vmem_limit_bytes=32 << 20),
        )(radial, azimuth)

    spec = P(None, "theta", "row", None)
    return jax.shard_map(
        per_device, mesh=mesh, in_specs=(spec,), out_specs=(spec, spec), check_vma=False
    )
```

time: 55.9 us -> 40.7 us (0.73)
  the two profiles are of different devices: /device:TPU:1 before, /device:TPU:16 now
where the time goes in v2:
time: 40.7 us; the launch traced here: 40.6 us
  Pallas kernels  39.9 us (98%)
  between operations  0.64 us (2%)
    pallas_call x1, Pallas kernels, per_device(): pl.pallas_call(functools.partial(tendencies, loop_size, shells), out_shap...  37.7 us
    pallas_call x1, Pallas kernels, per_device(): pl.pallas_call(write_out, out_shape=(result, result), in_specs=[vmem, vme...  2.23 us

profile of v2, /device:TPU:16, one launch (start us, length us, event | category | flops | bytes accessed | tf_op | source)
XLA Modules:
  0.0 40.6 jit_solution(13526669866898133674)
XLA Ops:
  0.6 37.7 %shard_map.30 = (bf16[3,8,384,128]{3,2,1,0:T(8,128)(2,1)S(1)}, bf16[3,8,384,128]{3,2,1,0:T(8,128)(2,1)S(1)}) custom-call(f32[3,8,384,128]{3,2,1,0:T(8,128)} %v.1), custom_call_target="tpu_custom_call" | custom-call | tf_op jit(solution)/shard_map/pallas_call | solution.py:273
  38.3 2.2 %shard_map.31 = (bf16[3,8,384,128]{3,2,1,0:T(8,128)(2,1)}, bf16[3,8,384,128]{3,2,1,0:T(8,128)(2,1)}) custom-call(bf16[3,8,384,128]{3,2,1,0:T(8,128)(2,1)S(1)} %get-tuple-element.4.radial_in, bf16[3,8,384,128]{3,2,1,0:T(8,128)(2,1)S(1)} %get-tuple-element.5.azimuth_in), custom_call_target="tpu_custom_call" | custom-call | tf_op jit(solution)/shard_map/pallas_call | solution.py:297

commit v3 on v2

--- a/solution.py
+++ b/solution.py
@@ -75,7 +75,7 @@
 
 def tendencies(
     loop_size, shells, v, radial, azimuth, ext, weights, stage, ghost,
-    own_sem, send_sem, recv_sem, ghost_send, ghost_recv, ready, turn,
+    own_sem, send_sem, recv_sem, ghost_send, ghost_recv, ready,
 ):
     width, rows = v.shape[1], v.shape[2]
     grid_r, grid_t = rows * shells, width * loop_size
@@ -94,19 +94,19 @@
     def signal(sem, at):
         pl.semaphore_signal(sem, inc=1, device_id=at, device_id_type=MESH)
 
+    odd = lax.rem(shell, 2) == 1
+    even = jnp.logical_not(odd)
     barrier = pltpu.get_barrier_semaphore()
     signal(barrier, (left, shell))
-    pl.when(not_outermost)(lambda: signal(barrier, (t, outer)))
+    pl.when(odd)(lambda: signal(barrier, (t, inner)))
+    pl.when(odd & not_outermost)(lambda: signal(barrier, (t, outer)))
     pl.when(first_half)(lambda: signal(barrier, (opposite, shell)))
 
     own = pltpu.make_async_copy(v, ext.at[:, pl.ds(2, width), pl.ds(PAD, rows), :], own_sem)
-    own.start()
-
-    partners = 1 + not_innermost.astype(jnp.int32) + second_half.astype(jnp.int32)
+
+    even_inner, even_outer = even & not_innermost, even & not_outermost
+    partners = 1 + even_inner.astype(jnp.int32) + even_outer.astype(jnp.int32) + second_half.astype(jnp.int32)
     pl.semaphore_wait(barrier, partners)
-    signal(ready.at[0], (right, shell))
-    pl.when(not_innermost)(lambda: signal(ready.at[1], (t, inner)))
-    pl.when(second_half)(lambda: signal(ready.at[2], (opposite, shell)))
 
     size = rows // PIECES
 
@@ -124,19 +124,22 @@
     rightward = [layers_copy(0, p) for p in range(PIECES)]
     leftward = [layers_copy(1, p) for p in range(PIECES)]
 
-    last_plane = lax.rem(t, RUN) == RUN - 1
-    even = lax.rem(shell, 2) == 0
-    waits_turn = last_plane & even
-    gives_turn = last_plane & jnp.logical_not(even)
-
-    @pl.when(jnp.logical_not(waits_turn))
-    def _():
-        for copy in rightward:
+    for copy in rightward:
+        copy.start()
+    signal(ready.at[0], (right, shell))
+    pl.when(even_inner)(lambda: signal(ready.at[1], (t, inner)))
+    pl.when(even_outer)(lambda: signal(ready.at[3], (t, outer)))
+    pl.when(second_half)(lambda: signal(ready.at[2], (opposite, shell)))
+    own.start()
+
+    first_plane = lax.rem(t, RUN) == 0
+
+    def send_leftward():
+        pl.semaphore_wait(ready.at[0], 1)
+        for copy in leftward:
             copy.start()
 
-    pl.semaphore_wait(ready.at[0], 1)
-    for copy in leftward:
-        copy.start()
+    pl.when(jnp.logical_not(first_plane))(send_leftward)
 
     own.wait()
 
@@ -161,15 +164,15 @@
     across = ghost_copy(0, 0, (opposite, shell))
     inward = ghost_copy(0, 1, (t, inner))
     outward = ghost_copy(1, 0, (t, outer))
+    pl.when(odd)(lambda: pl.semaphore_wait(ready.at[3], 1))
     pl.when(not_innermost)(inward.start)
-
-    @pl.when(not_outermost)
-    def _():
-        pl.semaphore_wait(ready.at[1], 1)
-        outward.start()
+    pl.when(odd & not_outermost)(lambda: pl.semaphore_wait(ready.at[1], 1))
+    pl.when(not_outermost)(outward.start)
 
     pl.when(first_half)(lambda: pl.semaphore_wait(ready.at[2], 1))
     pl.when(innermost)(across.start)
+
+    pl.when(first_plane)(send_leftward)
 
     blocks = rows // BLOCK
 
@@ -194,30 +197,6 @@
         radial_block(ext, weights, radial, m, END, half)
         radial_block(ext, weights, radial, m, END + half, half)
 
-    @pl.when(gives_turn)
-    def _():
-        for copy in rightward:
-            copy.wait_send()
-        signal(turn, (t, inner))
-
-    @pl.when(waits_turn)
-    def _():
-        pl.semaphore_wait(turn, 1)
-        for copy in rightward:
-            copy.start()
-
-    def edge_piece(copy, m, p):
-        copy.wait_recv()
-
-        @pl.loop(p * (size // BLOCK), (p + 1) * (size // BLOCK))
-        def _(b):
-            row = pl.multiple_of(b * BLOCK, BLOCK)
-            azimuth_block(ext, weights, azimuth, m, row, grid_r, grid_t)
-            azimuth_block(ext, weights, azimuth, m + 1, row, grid_r, grid_t)
-
-    for p in range(PIECES):
-        edge_piece(leftward[p], width - 2, p)
-
     across.wait_recv()
     pl.when(not_outermost)(inward.wait_recv)
     for c in range(3):
@@ -234,17 +213,23 @@
             radial_block(ext, weights, radial, m, 0, END)
             radial_block(ext, weights, radial, m, rows - END, END)
 
+    def edge_piece(copy, m, p):
+        copy.wait_recv()
+
+        @pl.loop(p * (size // BLOCK), (p + 1) * (size // BLOCK))
+        def _(b):
+            row = pl.multiple_of(b * BLOCK, BLOCK)
+            azimuth_block(ext, weights, azimuth, m, row, grid_r, grid_t)
+            azimuth_block(ext, weights, azimuth, m + 1, row, grid_r, grid_t)
+
+    for p in range(PIECES):
+        edge_piece(leftward[p], width - 2, p)
+
     for p in range(PIECES):
         edge_piece(rightward[p], 0, p)
 
-    for copy in leftward:
+    for copy in rightward + leftward:
         copy.wait_send()
-
-    @pl.when(jnp.logical_not(gives_turn))
-    def _():
-        for copy in rightward:
-            copy.wait_send()
-
     inward.wait_send()
     pl.when(not_outermost)(outward.wait_send)
 
@@ -285,8 +270,7 @@
                 dma((2, PIECES)),
                 dma((2,)),
                 dma((2,)),
-                pltpu.SemaphoreType.REGULAR((3,)),
-                pltpu.SemaphoreType.REGULAR,
+                pltpu.SemaphoreType.REGULAR((4,)),
             ],
             compiler_params=pltpu.CompilerParams(
                 collective_id=0, has_side_effects=True, vmem_limit_bytes=32 << 20

time: 40.7 us -> 38.6 us (0.948)
  the two profiles are of different devices: /device:TPU:16 before, /device:TPU:1 now
where the time goes in v3:
time: 38.6 us; the launch traced here: 38.5 us
  Pallas kernels  37.8 us (98%)
  between operations  0.64 us (2%)
    pallas_call x1, Pallas kernels, per_device(): pl.pallas_call(functools.partial(tendencies, loop_size, shells), out_shap...  35.6 us
    pallas_call x1, Pallas kernels, per_device(): pl.pallas_call(write_out, out_shape=(result, result), in_specs=[vmem, vme...  2.23 us

profile of v3, /device:TPU:1, one launch (start us, length us, event | category | flops | bytes accessed | tf_op | source)
XLA Modules:
  0.0 38.5 jit_solution(4993326529835619555)
XLA Ops:
  0.6 35.6 %shard_map.30 = (bf16[3,8,384,128]{3,2,1,0:T(8,128)(2,1)S(1)}, bf16[3,8,384,128]{3,2,1,0:T(8,128)(2,1)S(1)}) custom-call(f32[3,8,384,128]{3,2,1,0:T(8,128)} %v.1), custom_call_target="tpu_custom_call" | custom-call | tf_op jit(solution)/shard_map/pallas_call | solution.py:258
  36.2 2.2 %shard_map.31 = (bf16[3,8,384,128]{3,2,1,0:T(8,128)(2,1)}, bf16[3,8,384,128]{3,2,1,0:T(8,128)(2,1)}) custom-call(bf16[3,8,384,128]{3,2,1,0:T(8,128)(2,1)S(1)} %get-tuple-element.4.radial_in, bf16[3,8,384,128]{3,2,1,0:T(8,128)(2,1)S(1)} %get-tuple-element.5.azimuth_in), custom_call_target="tpu_custom_call" | custom-call | tf_op jit(solution)/shard_map/pallas_call | solution.py:281

commit v4 on v3

--- a/solution.py
+++ b/solution.py
@@ -12,6 +12,9 @@
 PAD = 8
 BLOCK = 32
 RUN = 8
+PLANE = 32
+RELAY = 7
+SHARE = 16
 END = 16
 PIECES = 4
 
@@ -75,7 +78,7 @@
 
 def tendencies(
     loop_size, shells, v, radial, azimuth, ext, weights, stage, ghost,
-    own_sem, send_sem, recv_sem, ghost_send, ghost_recv, ready,
+    own_sem, send_sem, recv_sem, ghost_send, ghost_recv, ready, passing, passing_ready, relay_send, relay_recv,
 ):
     width, rows = v.shape[1], v.shape[2]
     grid_r, grid_t = rows * shells, width * loop_size
@@ -102,34 +105,45 @@
     pl.when(odd & not_outermost)(lambda: signal(barrier, (t, outer)))
     pl.when(first_half)(lambda: signal(barrier, (opposite, shell)))
 
+    place = lax.rem(t, PLANE)
+    sender, receiver, relay = place == PLANE - 1, place == 0, place == RELAY
+    received_from, relayed_to = lax.rem(right + RELAY, loop_size), lax.max(t - RELAY, 0)
+    pl.when(receiver)(lambda: signal(barrier, (lax.rem(t + RELAY, loop_size), shell)))
+
     own = pltpu.make_async_copy(v, ext.at[:, pl.ds(2, width), pl.ds(PAD, rows), :], own_sem)
 
     even_inner, even_outer = even & not_innermost, even & not_outermost
     partners = 1 + even_inner.astype(jnp.int32) + even_outer.astype(jnp.int32) + second_half.astype(jnp.int32)
+    partners += relay.astype(jnp.int32)
     pl.semaphore_wait(barrier, partners)
 
     size = rows // PIECES
-
-    def layers_copy(d, p):
+    tail = rows - SHARE
+    leftward_rows = [(p * size, size) for p in range(PIECES)]
+    rightward_rows = [(tail, SHARE)] + [(p * size, min(size, tail - p * size)) for p in range(PIECES)]
+
+    def layers_copy(d, p, start, count):
         at, src, dst = ((right, width - 2, 0), (left, 0, width + 2))[d]
         return pltpu.make_async_remote_copy(
-            src_ref=v.at[:, pl.ds(src, 2), pl.ds(p * size, size), :],
-            dst_ref=ext.at[:, pl.ds(dst, 2), pl.ds(PAD + p * size, size), :],
+            src_ref=v.at[:, pl.ds(src, 2), pl.ds(start, count), :],
+            dst_ref=ext.at[:, pl.ds(dst, 2), pl.ds(PAD + start, count), :],
             send_sem=send_sem.at[d, p],
             recv_sem=recv_sem.at[d, p],
             device_id=(at, shell),
             device_id_type=MESH,
         )
 
-    rightward = [layers_copy(0, p) for p in range(PIECES)]
-    leftward = [layers_copy(1, p) for p in range(PIECES)]
-
-    for copy in rightward:
+    rightward = [layers_copy(0, p, *part) for p, part in enumerate(rightward_rows)]
+    leftward = [layers_copy(1, p, *part) for p, part in enumerate(leftward_rows)]
+
+    pl.when(jnp.logical_not(sender))(rightward[0].start)
+    for copy in rightward[1:]:
         copy.start()
     signal(ready.at[0], (right, shell))
     pl.when(even_inner)(lambda: signal(ready.at[1], (t, inner)))
     pl.when(even_outer)(lambda: signal(ready.at[3], (t, outer)))
     pl.when(second_half)(lambda: signal(ready.at[2], (opposite, shell)))
+    pl.when(relay)(lambda: signal(passing_ready.at[0], (relayed_to, shell)))
     own.start()
 
     first_plane = lax.rem(t, RUN) == 0
@@ -174,6 +188,12 @@
 
     pl.when(first_plane)(send_leftward)
 
+    @pl.when(receiver)
+    def _():
+        pl.semaphore_wait(passing_ready.at[0], 1)
+        signal(passing_ready.at[1], (left, shell))
+
+
     blocks = rows // BLOCK
 
     @pl.loop(0, blocks)
@@ -190,12 +210,39 @@
         for m in range(2, width - 2):
             azimuth_block(ext, weights, azimuth, m, row, grid_r, grid_t)
 
+    to_relay = pltpu.make_async_remote_copy(
+        src_ref=v.at[:, pl.ds(width - 2, 2), pl.ds(tail, SHARE), :],
+        dst_ref=passing,
+        send_sem=send_sem.at[0, 0],
+        recv_sem=relay_recv,
+        device_id=(received_from, shell),
+        device_id_type=MESH,
+    )
+    from_relay = pltpu.make_async_remote_copy(
+        src_ref=passing,
+        dst_ref=ext.at[:, pl.ds(0, 2), pl.ds(PAD + tail, SHARE), :],
+        send_sem=relay_send,
+        recv_sem=recv_sem.at[0, 0],
+        device_id=(relayed_to, shell),
+        device_id_type=MESH,
+    )
+
+    @pl.when(sender)
+    def _():
+        pl.semaphore_wait(passing_ready.at[1], 1)
+        to_relay.start()
+
     half = rows // 2 - END
 
     @pl.loop(0, width)
     def _(m):
         radial_block(ext, weights, radial, m, END, half)
         radial_block(ext, weights, radial, m, END + half, half)
+
+    @pl.when(relay)
+    def _():
+        to_relay.wait_recv()
+        from_relay.start()
 
     across.wait_recv()
     pl.when(not_outermost)(inward.wait_recv)
@@ -213,21 +260,23 @@
             radial_block(ext, weights, radial, m, 0, END)
             radial_block(ext, weights, radial, m, rows - END, END)
 
-    def edge_piece(copy, m, p):
-        copy.wait_recv()
-
-        @pl.loop(p * (size // BLOCK), (p + 1) * (size // BLOCK))
+    def edge_rows(m, start, count):
+        @pl.loop(start // BLOCK, (start + count) // BLOCK)
         def _(b):
             row = pl.multiple_of(b * BLOCK, BLOCK)
             azimuth_block(ext, weights, azimuth, m, row, grid_r, grid_t)
             azimuth_block(ext, weights, azimuth, m + 1, row, grid_r, grid_t)
 
-    for p in range(PIECES):
-        edge_piece(leftward[p], width - 2, p)
-
-    for p in range(PIECES):
-        edge_piece(rightward[p], 0, p)
-
+    for copy, part in zip(leftward, leftward_rows):
+        copy.wait_recv()
+        edge_rows(width - 2, *part)
+
+    rightward[0].wait_recv()
+    for copy, part in zip(rightward[1:], rightward_rows[1:]):
+        copy.wait_recv()
+        edge_rows(0, part[0], size)
+
+    pl.when(relay)(from_relay.wait_send)
     for copy in rightward + leftward:
         copy.wait_send()
     inward.wait_send()
@@ -266,11 +315,15 @@
                 pltpu.VMEM((2, 6 * width, planes), jnp.float32),
                 pltpu.VMEM((2, 6 * width, planes), jnp.float32),
                 dma,
-                dma((2, PIECES)),
-                dma((2, PIECES)),
+                dma((2, PIECES + 1)),
+                dma((2, PIECES + 1)),
                 dma((2,)),
                 dma((2,)),
                 pltpu.SemaphoreType.REGULAR((4,)),
+                pltpu.VMEM((3, 2, SHARE, planes), jnp.float32),
+                pltpu.SemaphoreType.REGULAR((2,)),
+                dma,
+                dma,
             ],
             compiler_params=pltpu.CompilerParams(
                 collective_id=0, has_side_effects=True, vmem_limit_bytes=32 << 20

time: 38.6 us -> 37.8 us (0.979)
  Pallas kernels: 37.8 us -> 36.9 us
    pallas_call x1, Pallas kernels: 35.6 us -> 34.7 us  [per_device(): pl.pallas_call(functools.partial(tendencies, loop_size, shells), out_shap...]
where the time goes in v4:
time: 37.8 us; the launch traced here: 37.5 us
  Pallas kernels  36.9 us (98%)
  between operations  0.64 us (2%)
    pallas_call x1, Pallas kernels, per_device(): pl.pallas_call(functools.partial(tendencies, loop_size, shells), out_shap...  34.7 us
    pallas_call x1, Pallas kernels, per_device(): pl.pallas_call(write_out, out_shape=(result, result), in_specs=[vmem, vme...  2.23 us

profile of v4, /device:TPU:1, one launch (start us, length us, event | category | flops | bytes accessed | tf_op | source)
XLA Modules:
  0.0 37.5 jit_solution(17867139413873434728)
XLA Ops:
  0.6 34.7 %shard_map.30 = (bf16[3,8,384,128]{3,2,1,0:T(8,128)(2,1)S(1)}, bf16[3,8,384,128]{3,2,1,0:T(8,128)(2,1)S(1)}) custom-call(f32[3,8,384,128]{3,2,1,0:T(8,128)} %v.1), custom_call_target="tpu_custom_call" | custom-call | tf_op jit(solution)/shard_map/pallas_call | solution.py:307
  35.3 2.2 %shard_map.31 = (bf16[3,8,384,128]{3,2,1,0:T(8,128)(2,1)}, bf16[3,8,384,128]{3,2,1,0:T(8,128)(2,1)}) custom-call(bf16[3,8,384,128]{3,2,1,0:T(8,128)(2,1)S(1)} %get-tuple-element.4.radial_in, bf16[3,8,384,128]{3,2,1,0:T(8,128)(2,1)S(1)} %get-tuple-element.5.azimuth_in), custom_call_target="tpu_custom_call" | custom-call | tf_op jit(solution)/shard_map/pallas_call | solution.py:334

commit v5 on v3

--- a/solution.py
+++ b/solution.py
@@ -12,6 +12,12 @@
 PAD = 8
 BLOCK = 32
 RUN = 8
+PLANE = 32
+RELAYS = (7,)
+BACK = 24
+SHARE = 24
+BACK_SHARE = 24
+EARLY = 2
 END = 16
 PIECES = 4
 
@@ -75,7 +81,7 @@
 
 def tendencies(
     loop_size, shells, v, radial, azimuth, ext, weights, stage, ghost,
-    own_sem, send_sem, recv_sem, ghost_send, ghost_recv, ready,
+    own_sem, send_sem, recv_sem, ghost_send, ghost_recv, ready, passing, passing_ready, back_ready, relay_send, relay_recv,
 ):
     width, rows = v.shape[1], v.shape[2]
     grid_r, grid_t = rows * shells, width * loop_size
@@ -102,42 +108,110 @@
     pl.when(odd & not_outermost)(lambda: signal(barrier, (t, outer)))
     pl.when(first_half)(lambda: signal(barrier, (opposite, shell)))
 
+    place = lax.rem(t, PLANE)
+    sender, receiver = place == PLANE - 1, place == 0
+    relays = [place == relay for relay in RELAYS]
+    relaying = functools.reduce(jnp.logical_or, relays)
+    back_relay = place == BACK
+    to_back = lax.rem(t + loop_size - PLANE + BACK, loop_size)
+    back_from = lax.rem(t + PLANE - BACK, loop_size)
+    last = lax.rem(t + PLANE - 1 - BACK, loop_size)
+    known_back = lax.max(t - PLANE + 1 + BACK, 0)
+
+    @pl.when(receiver)
+    def _():
+        for relay in RELAYS:
+            signal(barrier, (lax.rem(t + relay, loop_size), shell))
+
+    @pl.when(back_relay)
+    def _():
+        signal(barrier, (back_from, shell))
+        signal(barrier, (last, shell))
+
     own = pltpu.make_async_copy(v, ext.at[:, pl.ds(2, width), pl.ds(PAD, rows), :], own_sem)
 
     even_inner, even_outer = even & not_innermost, even & not_outermost
     partners = 1 + even_inner.astype(jnp.int32) + even_outer.astype(jnp.int32) + second_half.astype(jnp.int32)
+    partners += (relaying | receiver | sender).astype(jnp.int32)
     pl.semaphore_wait(barrier, partners)
+    signal(ready.at[0], (right, shell))
 
     size = rows // PIECES
-
-    def layers_copy(d, p):
+    tail = rows - len(RELAYS) * SHARE
+    back_tail = rows - BACK_SHARE
+    leftward_rows = [(back_tail, BACK_SHARE)] + [(p * size, min(size, back_tail - p * size)) for p in range(PIECES)]
+    rightward_rows = [(tail + k * SHARE, SHARE) for k in range(len(RELAYS))]
+    rightward_rows += [(p * size, min(size, tail - p * size)) for p in range(PIECES)]
+
+    def layers_copy(d, p, start, count):
         at, src, dst = ((right, width - 2, 0), (left, 0, width + 2))[d]
         return pltpu.make_async_remote_copy(
-            src_ref=v.at[:, pl.ds(src, 2), pl.ds(p * size, size), :],
-            dst_ref=ext.at[:, pl.ds(dst, 2), pl.ds(PAD + p * size, size), :],
+            src_ref=v.at[:, pl.ds(src, 2), pl.ds(start, count), :],
+            dst_ref=ext.at[:, pl.ds(dst, 2), pl.ds(PAD + start, count), :],
             send_sem=send_sem.at[d, p],
             recv_sem=recv_sem.at[d, p],
             device_id=(at, shell),
             device_id_type=MESH,
         )
 
-    rightward = [layers_copy(0, p) for p in range(PIECES)]
-    leftward = [layers_copy(1, p) for p in range(PIECES)]
-
-    for copy in rightward:
+    rightward = [layers_copy(0, p, *part) for p, part in enumerate(rightward_rows)]
+    leftward = [layers_copy(1, p, *part) for p, part in enumerate(leftward_rows)]
+
+    to_back_relay = pltpu.make_async_remote_copy(
+        src_ref=v.at[:, pl.ds(0, 2), pl.ds(back_tail, BACK_SHARE), :],
+        dst_ref=passing.at[:, :, pl.ds(0, BACK_SHARE), :],
+        send_sem=send_sem.at[1, 0],
+        recv_sem=relay_recv,
+        device_id=(to_back, shell),
+        device_id_type=MESH,
+    )
+    from_back_relay = pltpu.make_async_remote_copy(
+        src_ref=passing.at[:, :, pl.ds(0, BACK_SHARE), :],
+        dst_ref=ext.at[:, pl.ds(width + 2, 2), pl.ds(PAD + back_tail, BACK_SHARE), :],
+        send_sem=relay_send,
+        recv_sem=recv_sem.at[1, 0],
+        device_id=(last, shell),
+        device_id_type=MESH,
+    )
+
+    @pl.when(jnp.logical_not(sender))
+    def _():
+        for copy in rightward[: len(RELAYS)]:
+            copy.start()
+
+    takes_part = sender | relaying
+    early_right, late_right = rightward[len(RELAYS) : len(RELAYS) + EARLY], rightward[len(RELAYS) + EARLY :]
+    early_left, late_left = leftward[1:2], leftward[2:]
+    for copy in early_right:
         copy.start()
-    signal(ready.at[0], (right, shell))
+
+    @pl.when(jnp.logical_not(takes_part))
+    def _():
+        for copy in late_right:
+            copy.start()
+
+    pl.when(sender)(lambda: signal(back_ready, (known_back, shell)))
     pl.when(even_inner)(lambda: signal(ready.at[1], (t, inner)))
     pl.when(even_outer)(lambda: signal(ready.at[3], (t, outer)))
     pl.when(second_half)(lambda: signal(ready.at[2], (opposite, shell)))
+    for k, mine in enumerate(relays):
+        pl.when(mine)(lambda: signal(passing_ready.at[k], (lax.max(t - RELAYS[k], 0), shell)))
     own.start()
+
+    pl.when(receiver)(to_back_relay.start)
 
     first_plane = lax.rem(t, RUN) == 0
 
     def send_leftward():
         pl.semaphore_wait(ready.at[0], 1)
-        for copy in leftward:
+        pl.when(jnp.logical_not(receiver))(leftward[0].start)
+        for copy in early_left:
             copy.start()
+
+        @pl.when(jnp.logical_not(sender))
+        def _():
+            for copy in late_left:
+                copy.start()
 
     pl.when(jnp.logical_not(first_plane))(send_leftward)
 
@@ -172,7 +246,20 @@
     pl.when(first_half)(lambda: pl.semaphore_wait(ready.at[2], 1))
     pl.when(innermost)(across.start)
 
+    @pl.when(back_relay)
+    def _():
+        to_back_relay.wait_recv()
+        pl.semaphore_wait(back_ready, 1)
+        from_back_relay.start()
+
     pl.when(first_plane)(send_leftward)
+
+    @pl.when(receiver)
+    def _():
+        for k in range(len(RELAYS)):
+            pl.semaphore_wait(passing_ready.at[k], 1)
+        signal(passing_ready.at[len(RELAYS)], (left, shell))
+
 
     blocks = rows // BLOCK
 
@@ -190,12 +277,52 @@
         for m in range(2, width - 2):
             azimuth_block(ext, weights, azimuth, m, row, grid_r, grid_t)
 
+    def to_relay(k):
+        return pltpu.make_async_remote_copy(
+            src_ref=v.at[:, pl.ds(width - 2, 2), pl.ds(tail + k * SHARE, SHARE), :],
+            dst_ref=passing.at[:, :, pl.ds(0, SHARE), :],
+            send_sem=send_sem.at[0, k],
+            recv_sem=relay_recv,
+            device_id=(lax.rem(right + RELAYS[k], loop_size), shell),
+            device_id_type=MESH,
+        )
+
+    def from_relay(k):
+        return pltpu.make_async_remote_copy(
+            src_ref=passing.at[:, :, pl.ds(0, SHARE), :],
+            dst_ref=ext.at[:, pl.ds(0, 2), pl.ds(PAD + tail + k * SHARE, SHARE), :],
+            send_sem=relay_send,
+            recv_sem=recv_sem.at[0, k],
+            device_id=(lax.max(t - RELAYS[k], 0), shell),
+            device_id_type=MESH,
+        )
+
+    @pl.when(sender)
+    def _():
+        pl.semaphore_wait(passing_ready.at[len(RELAYS)], 1)
+        for k in range(len(RELAYS)):
+            to_relay(k).start()
+        for copy in late_right + late_left:
+            copy.start()
+
     half = rows // 2 - END
 
     @pl.loop(0, width)
     def _(m):
         radial_block(ext, weights, radial, m, END, half)
         radial_block(ext, weights, radial, m, END + half, half)
+
+    for k, mine in enumerate(relays):
+
+        @pl.when(mine)
+        def _():
+            to_relay(k).wait_recv()
+            from_relay(k).start()
+
+    @pl.when(relaying)
+    def _():
+        for copy in late_right:
+            copy.start()
 
     across.wait_recv()
     pl.when(not_outermost)(inward.wait_recv)
@@ -213,21 +340,27 @@
             radial_block(ext, weights, radial, m, 0, END)
             radial_block(ext, weights, radial, m, rows - END, END)
 
-    def edge_piece(copy, m, p):
-        copy.wait_recv()
-
-        @pl.loop(p * (size // BLOCK), (p + 1) * (size // BLOCK))
+    def edge_rows(m, start, count):
+        @pl.loop(start // BLOCK, (start + count) // BLOCK)
         def _(b):
             row = pl.multiple_of(b * BLOCK, BLOCK)
             azimuth_block(ext, weights, azimuth, m, row, grid_r, grid_t)
             azimuth_block(ext, weights, azimuth, m + 1, row, grid_r, grid_t)
 
-    for p in range(PIECES):
-        edge_piece(leftward[p], width - 2, p)
-
-    for p in range(PIECES):
-        edge_piece(rightward[p], 0, p)
-
+    leftward[0].wait_recv()
+    for copy, part in zip(leftward[1:], leftward_rows[1:]):
+        copy.wait_recv()
+        edge_rows(width - 2, part[0], size)
+
+    for copy in rightward[: len(RELAYS)]:
+        copy.wait_recv()
+    for copy, part in zip(rightward[len(RELAYS) :], rightward_rows[len(RELAYS) :]):
+        copy.wait_recv()
+        edge_rows(0, part[0], size)
+
+    for k, mine in enumerate(relays):
+        pl.when(mine)(from_relay(k).wait_send)
+    pl.when(back_relay)(from_back_relay.wait_send)
     for copy in rightward + leftward:
         copy.wait_send()
     inward.wait_send()
@@ -266,11 +399,16 @@
                 pltpu.VMEM((2, 6 * width, planes), jnp.float32),
                 pltpu.VMEM((2, 6 * width, planes), jnp.float32),
                 dma,
-                dma((2, PIECES)),
-                dma((2, PIECES)),
+                dma((2, PIECES + 1)),
+                dma((2, PIECES + 1)),
                 dma((2,)),
                 dma((2,)),
                 pltpu.SemaphoreType.REGULAR((4,)),
+                pltpu.VMEM((3, 2, max(SHARE, BACK_SHARE), planes), jnp.float32),
+                pltpu.SemaphoreType.REGULAR((len(RELAYS) + 1,)),
+                pltpu.SemaphoreType.REGULAR,
+                dma,
+                dma,
             ],
             compiler_params=pltpu.CompilerParams(
                 collective_id=0, has_side_effects=True, vmem_limit_bytes=32 << 20

time: 38.6 us -> 37.3 us (0.966)
  Pallas kernels: 37.8 us -> 36.4 us
    pallas_call x1, Pallas kernels: 35.6 us -> 34.2 us  [per_device(): pl.pallas_call(functools.partial(tendencies, loop_size, shells), out_shap...]
where the time goes in v5:
time: 37.3 us; the launch traced here: 37.1 us
  Pallas kernels  36.4 us (98%)
  between operations  0.64 us (2%)
    pallas_call x1, Pallas kernels, per_device(): pl.pallas_call(functools.partial(tendencies, loop_size, shells), out_shap...  34.2 us
    pallas_call x1, Pallas kernels, per_device(): pl.pallas_call(write_out, out_shape=(result, result), in_specs=[vmem, vme...  2.23 us

profile of v5, /device:TPU:1, one launch (start us, length us, event | category | flops | bytes accessed | tf_op | source)
XLA Modules:
  0.0 37.1 jit_solution(14505239813823287714)
XLA Ops:
  0.6 34.2 %shard_map.30 = (bf16[3,8,384,128]{3,2,1,0:T(8,128)(2,1)S(1)}, bf16[3,8,384,128]{3,2,1,0:T(8,128)(2,1)S(1)}) custom-call(f32[3,8,384,128]{3,2,1,0:T(8,128)} %v.1), custom_call_target="tpu_custom_call" | custom-call | tf_op jit(solution)/shard_map/pallas_call | solution.py:391
  34.8 2.2 %shard_map.31 = (bf16[3,8,384,128]{3,2,1,0:T(8,128)(2,1)}, bf16[3,8,384,128]{3,2,1,0:T(8,128)(2,1)}) custom-call(bf16[3,8,384,128]{3,2,1,0:T(8,128)(2,1)S(1)} %get-tuple-element.4.radial_in, bf16[3,8,384,128]{3,2,1,0:T(8,128)(2,1)S(1)} %get-tuple-element.5.azimuth_in), custom_call_target="tpu_custom_call" | custom-call | tf_op jit(solution)/shard_map/pallas_call | solution.py:419

commit v6 on v5

--- a/solution.py
+++ b/solution.py
@@ -17,7 +17,7 @@
 BACK = 24
 SHARE = 24
 BACK_SHARE = 24
-EARLY = 2
+EARLY = 3
 END = 16
 PIECES = 4
 

time: 37.3 us -> 37.3 us (level)
  no operation moved by 1% of the time
where the time goes in v6:
time: 37.3 us; the launch traced here: 37.1 us
  Pallas kernels  36.4 us (98%)
  between operations  0.64 us (2%)
    pallas_call x1, Pallas kernels, per_device(): pl.pallas_call(functools.partial(tendencies, loop_size, shells), out_shap...  34.2 us
    pallas_call x1, Pallas kernels, per_device(): pl.pallas_call(write_out, out_shape=(result, result), in_specs=[vmem, vme...  2.23 us

profile of v6, /device:TPU:1, one launch (start us, length us, event | category | flops | bytes accessed | tf_op | source)
XLA Modules:
  0.0 37.1 jit_solution(982557663158337313)
XLA Ops:
  0.6 34.2 %shard_map.30 = (bf16[3,8,384,128]{3,2,1,0:T(8,128)(2,1)S(1)}, bf16[3,8,384,128]{3,2,1,0:T(8,128)(2,1)S(1)}) custom-call(f32[3,8,384,128]{3,2,1,0:T(8,128)} %v.1), custom_call_target="tpu_custom_call" | custom-call | tf_op jit(solution)/shard_map/pallas_call | solution.py:391
  34.8 2.2 %shard_map.31 = (bf16[3,8,384,128]{3,2,1,0:T(8,128)(2,1)}, bf16[3,8,384,128]{3,2,1,0:T(8,128)(2,1)}) custom-call(bf16[3,8,384,128]{3,2,1,0:T(8,128)(2,1)S(1)} %get-tuple-element.4.radial_in, bf16[3,8,384,128]{3,2,1,0:T(8,128)(2,1)S(1)} %get-tuple-element.5.azimuth_in), custom_call_target="tpu_custom_call" | custom-call | tf_op jit(solution)/shard_map/pallas_call | solution.py:419

commit v7 on v5

--- a/solution.py
+++ b/solution.py
@@ -370,8 +370,7 @@
 def write_out(radial_in, azimuth_in, radial, azimuth, sems):
     copies = []
     for k, (src, dst) in enumerate(((radial_in, radial), (azimuth_in, azimuth))):
-        for c in range(3):
-            copies.append(pltpu.make_async_copy(src.at[c], dst.at[c], sems.at[k, c]))
+        copies.append(pltpu.make_async_copy(src, dst, sems.at[k]))
     for copy in copies:
         copy.start()
     for copy in copies:
@@ -421,7 +420,7 @@
             out_shape=(result, result),
             in_specs=[vmem, vmem],
             out_specs=(hbm, hbm),
-            scratch_shapes=[dma((2, 3))],
+            scratch_shapes=[dma((2,))],
             compiler_params=pltpu.CompilerParams(vmem_limit_bytes=32 << 20),
         )(radial, azimuth)
 

time: 37.3 us -> 37.2 us (level)
  no operation moved by 1% of the time
where the time goes in v7:
time: 37.2 us; the launch traced here: 37 us
  Pallas kernels  36.4 us (98%)
  between operations  0.64 us (2%)
    pallas_call x1, Pallas kernels, per_device(): pl.pallas_call(functools.partial(tendencies, loop_size, shells), out_shap...  34.2 us
    pallas_call x1, Pallas kernels, per_device(): pl.pallas_call(write_out, out_shape=(result, result), in_specs=[vmem, vme...  2.2 us

profile of v7, /device:TPU:1, one launch (start us, length us, event | category | flops | bytes accessed | tf_op | source)
XLA Modules:
  0.0 37.0 jit_solution(17016207219818102452)
XLA Ops:
  0.6 34.2 %shard_map.30 = (bf16[3,8,384,128]{3,2,1,0:T(8,128)(2,1)S(1)}, bf16[3,8,384,128]{3,2,1,0:T(8,128)(2,1)S(1)}) custom-call(f32[3,8,384,128]{3,2,1,0:T(8,128)} %v.1), custom_call_target="tpu_custom_call" | custom-call | tf_op jit(solution)/shard_map/pallas_call | solution.py:390
  34.8 2.2 %shard_map.31 = (bf16[3,8,384,128]{3,2,1,0:T(8,128)(2,1)}, bf16[3,8,384,128]{3,2,1,0:T(8,128)(2,1)}) custom-call(bf16[3,8,384,128]{3,2,1,0:T(8,128)(2,1)S(1)} %get-tuple-element.4.radial_in, bf16[3,8,384,128]{3,2,1,0:T(8,128)(2,1)S(1)} %get-tuple-element.5.azimuth_in), custom_call_target="tpu_custom_call" | custom-call | tf_op jit(solution)/shard_map/pallas_call | solution.py:418
